TPU v7x, 32 devices: a whole 2x2x4 slice. The times are simulated.
32 devices in a mesh: row: 8 (over z, y), col: 4 (over x, core).
Axes of the slice: x: 2, y: 2, z: 4, core: 2. Of those that a mesh axis runs over, the one named last changes fastest.
Arguments:
- coeff: bfloat16 [3072, 1536], P('row', 'col'), may hold values from -6 to 6
- bank: bfloat16 [16, 384, 384], replicated, may hold values from -0.09375 to 0.09375
- alpha_tiles: int32 [8, 24], replicated, may hold values from 0 to 7
- alpha_blocks: int32 [8, 24], replicated, may hold values from 0 to 15
- alpha_count: int32 [8], replicated, may hold values from 2 to 24, as said below
- beta_tiles: int32 [4, 24], replicated, may hold values from 0 to 3
- beta_blocks: int32 [4, 24], replicated, may hold values from 0 to 15
- beta_count: int32 [4], replicated, may hold values from 2 to 24, as said below
Outputs:
- sigma: float32 [3072, 1536], P('row', 'col')
Inputs may be any that keep to these rules, and one draw needn't show every extreme that they name: `alpha_count`: every value lies in 2 to 24; some tile has all 24 slots live. `beta_count`: every value lies in 2 to 24; some tile has all 24 slots live.
All inputs are finite; a program needn't handle non-finite values.
Results may differ from a plain program's by a relative error of at most 0.0003.
Values may be sent and summed in bfloat16 or wider, within the bound.
A program may use at most 64 MiB of HBM per device.

v0:
```python
import functools

import jax
import jax.numpy as jnp
from jax import lax
from jax.experimental import pallas as pl
from jax.experimental.pallas import tpu as pltpu
from jax.sharding import PartitionSpec as P

MESH = pl.DeviceIdType.MESH
LATE = 1


def kernel(
    n_row, n_col,
    a_tiles, a_blocks, a_count, b_tiles, b_blocks, b_count,
    coeff, bank_hbm, out,
    rows, cols, bank, local_sem, row_send, row_recv, col_send, col_recv,
):
    tile = coeff.shape[0]
    half = tile // 2
    slots = a_tiles.shape[1]
    depth, width = n_row // 2, n_col // 2
    row, col = lax.axis_index("row"), lax.axis_index("col")
    z, y = row // 2, row % 2
    x, core = col // 2, col % 2
    mate = row + 1 - 2 * y
    twin = col + 1 - 2 * core

    def part(ref, which, h):
        return ref.at[which, pl.ds(h * half, half), :]

    def own(h):
        return coeff.at[pl.ds(h * half, half), :]

    def row_copy(src, which, h, way, target):
        return pltpu.make_async_remote_copy(
            src_ref=src, dst_ref=part(rows, which, h),
            send_sem=row_send.at[way, which, h], recv_sem=row_recv.at[which, h],
            device_id=(target, col), device_id_type=MESH,
        )

    def col_copy(src, which, h, way, target):
        return pltpu.make_async_remote_copy(
            src_ref=src, dst_ref=part(cols, which, h),
            send_sem=col_send.at[way, which, h], recv_sem=col_recv.at[which, h],
            device_id=(row, target), device_id_type=MESH,
        )

    def arrived(which, h):
        row_copy(own(h), which, h, 0, mate).wait_recv()

    bank_copy = pltpu.make_async_copy(bank_hbm, bank, local_sem.at[0])
    bank_copy.start()
    own_row = pltpu.make_async_copy(coeff, rows.at[row], local_sem.at[1])
    own_row.start()
    own_col = pltpu.make_async_copy(coeff, cols.at[col], local_sem.at[2])
    own_col.start()

    has_up, has_down = z + 1 < depth, z >= 1

    barrier = pltpu.get_barrier_semaphore()

    def greet(r, c):
        pl.semaphore_signal(barrier, inc=1, device_id=(r, c), device_id_type=MESH)

    @pl.when(has_up)
    def _():
        greet(row + 2, col)

    @pl.when(has_down)
    def _():
        greet(row - 2, col)

    greet(mate, col)
    greet(row, twin)
    for step in range(1, width):
        greet(row, lax.rem(x + step, width) * 2 + core)
    neighbours = 1 + width + has_up.astype(jnp.int32) + has_down.astype(jnp.int32)
    pl.semaphore_wait(barrier, neighbours)

    UP, DOWN, SIDE = 0, 1, 2

    for h in (0, 1):
        @pl.when(has_up)
        def _():
            row_copy(own(h), row, h, UP, row + 2).start()

        @pl.when(has_down)
        def _():
            row_copy(own(h), row, h, DOWN, row - 2).start()

        row_copy(own(h), row, h, SIDE, mate).start()
        for step in range(1, width):
            col_copy(own(h), col, h, step, lax.rem(x + step, width) * 2 + core).start()
        col_copy(own(h), col, h, 0, twin).start()

    def pass_rows(d, h):
        below, above = row - 2 * d, row + 2 * d

        @pl.when(z >= d)
        def _():
            arrived(below, h)

            @pl.when(has_up)
            def _():
                row_copy(part(rows, below, h), below, h, UP, row + 2).start()

            if d != 1 or h != LATE:
                row_copy(part(rows, below, h), below, h, SIDE, mate).start()

        @pl.when(z + d < depth)
        def _():
            arrived(above, h)

            @pl.when(has_down)
            def _():
                row_copy(part(rows, above, h), above, h, DOWN, row - 2).start()

            if d != 1 or h != LATE:
                row_copy(part(rows, above, h), above, h, SIDE, mate).start()

    def pass_mate():
        arrived(mate, LATE)

        @pl.when(has_up)
        def _():
            row_copy(part(rows, mate, LATE), mate, LATE, UP, row + 2).start()

        @pl.when(has_down)
        def _():
            row_copy(part(rows, mate, LATE), mate, LATE, DOWN, row - 2).start()

    def pass_cols(h):
        for step in range(1, width):
            source = lax.rem(x + width - step, width) * 2 + core
            col_copy(own(h), source, h, 0, twin).wait_recv()
            col_copy(part(cols, source, h), source, h, 0, twin).start()

    pass_rows(1, 0)
    pass_cols(0)
    pass_rows(1, 1)
    pass_cols(1)
    if depth > 2:
        pass_rows(2, 0)

    own_col.wait()
    bank_copy.wait()
    for h in (0, 1):
        for step in range(width):
            source = lax.rem(x + step, width) * 2 + 1 - core
            col_copy(own(h), source, h, 0, twin).wait_recv()
    out[...] = jnp.zeros_like(out)
    b_live = b_count[col]

    def add_beta(slot):
        piece = cols[b_tiles[col, slot]]
        block = bank[b_blocks[col, slot]]
        live = jnp.where(slot < b_live, 1.0, 0.0).astype(jnp.float32)
        out[...] += live * lax.dot_general(
            piece, block, (((1,), (1,)), ((), ())), preferred_element_type=jnp.float32
        )

    def beta_range(low, high):
        def body(slot, carry):
            add_beta(slot)
            return carry
        lax.fori_loop(low, high, body, 0)

    beta_range(0, slots // 3)
    if depth > 2:
        pass_rows(2, 1)
    else:
        pass_mate()
    beta_range(slots // 3, 2 * slots // 3)
    if depth > 2:
        pass_mate()
    for d in range(3, depth):
        pass_rows(d, 0)
        if d == 3:
            beta_range(2 * slots // 3, slots)
        pass_rows(d, 1)
    if depth <= 3:
        beta_range(2 * slots // 3, slots)

    own_row.wait()
    arrived(mate, 1 - LATE)
    for d in range(1, depth):
        for h in (0, 1):
            @pl.when(z >= d)
            def _():
                arrived(mate - 2 * d, h)

            @pl.when(z + d < depth)
            def _():
                arrived(mate + 2 * d, h)

    a_live = a_count[row]

    def add_alpha(slot, carry):
        piece = rows[a_tiles[row, slot]]
        block = bank[a_blocks[row, slot]]
        live = jnp.where(slot < a_live, 1.0, 0.0).astype(jnp.float32)
        out[...] += live * jnp.dot(block, piece, preferred_element_type=jnp.float32)
        return carry

    lax.fori_loop(0, slots, add_alpha, 0)

    def sent_row(which, h, way):
        row_copy(own(h), which, h, way, mate).wait_send()

    for h in (0, 1):
        @pl.when(has_up)
        def _():
            sent_row(row, h, UP)

        @pl.when(has_down)
        def _():
            sent_row(row, h, DOWN)

        sent_row(row, h, SIDE)
        for step in range(1, width):
            col_copy(own(h), col, h, step, twin).wait_send()
        for step in range(width):
            source = lax.rem(x + step, width) * 2 + core
            col_copy(own(h), source, h, 0, twin).wait_send()
        for d in range(1, depth):
            @pl.when(z >= d)
            def _():
                @pl.when(has_up)
                def _():
                    sent_row(row - 2 * d, h, UP)

                if d != 1 or h != LATE:
                    sent_row(row - 2 * d, h, SIDE)

            @pl.when(z + d < depth)
            def _():
                @pl.when(has_down)
                def _():
                    sent_row(row + 2 * d, h, DOWN)

                if d != 1 or h != LATE:
                    sent_row(row + 2 * d, h, SIDE)

    @pl.when(has_up)
    def _():
        sent_row(mate, LATE, UP)

    @pl.when(has_down)
    def _():
        sent_row(mate, LATE, DOWN)


def solution(mesh):
    n_row, n_col = mesh.shape["row"], mesh.shape["col"]

    def local(coeff, bank, a_tiles, a_blocks, a_count, b_tiles, b_blocks, b_count):
        tile = coeff.shape[0]
        flops = 2 * (a_tiles.shape[1] + b_tiles.shape[1]) * tile**3
        return pl.pallas_call(
            functools.partial(kernel, n_row, n_col),
            out_shape=jax.ShapeDtypeStruct((tile, tile), jnp.float32),
            in_specs=[pl.BlockSpec(memory_space=pltpu.SMEM)] * 6
            + [pl.BlockSpec(memory_space=pltpu.HBM)] * 2,
            out_specs=pl.BlockSpec(memory_space=pltpu.VMEM),
            scratch_shapes=[
                pltpu.VMEM((n_row, tile, tile), coeff.dtype),
                pltpu.VMEM((n_col, tile, tile), coeff.dtype),
                pltpu.VMEM(bank.shape, bank.dtype),
                pltpu.SemaphoreType.DMA((3,)),
                pltpu.SemaphoreType.DMA((3, n_row, 2)),
                pltpu.SemaphoreType.DMA((n_row, 2)),
                pltpu.SemaphoreType.DMA((max(1, n_col // 2), n_col, 2)),
                pltpu.SemaphoreType.DMA((n_col, 2)),
            ],
            compiler_params=pltpu.CompilerParams(
                collective_id=0, has_side_effects=True, vmem_limit_bytes=62 * 1024 * 1024
            ),
            cost_estimate=pl.CostEstimate(
                flops=flops, bytes_accessed=bank.size * 2 + tile * tile * 6, transcendentals=0
            ),
        )(a_tiles, a_blocks, a_count, b_tiles, b_blocks, b_count, coeff, bank)

    return jax.shard_map(
        local,
        mesh=mesh,
        in_specs=(P("row", "col"), P(), P(), P(), P(), P(), P(), P()),
        out_specs=P("row", "col"),
        check_vma=False,
    )
```

profile of v0, /device:TPU:0, one launch (start us, length us, event | category | flops | bytes accessed | tf_op | source)
XLA Modules:
  0.0 42.7 jit_solution(16480889060231904009)
XLA Ops:
  0.0 40.7 %shard_map.82 = f32[384,384]{1,0:T(8,128)} custom-call(s32[8,24]{1,0:T(8,128)} %a_tiles.1, s32[8,24]{1,0:T(8,128)} %a_blocks.1, s32[8]{0:T(128)} %a_count.1, s32[4,24]{1,0:T(4,128)} %b_tiles.1, s32[4,24]{1,0:T(4,128)} %b_blocks.1, s32[4]{0:T(128)} %b_count.1, bf16[384,384]{1,0:T(8,128)(2,1)} %coeff.1, bf16[16,384,384]{2,1,0:T(8,128)(2,1)} %bank_hbm.1), custom_call_target="tpu_custom_call" | custom-call | flops 5435817984 | bytes 5603328 | tf_op jit(solution)/shard_map/pallas_call | solution.py:261
  40.7 1.9 %copy.10 = f32[384,384]{1,0:T(8,128)} copy(f32[384,384]{1,0:T(8,128)} %shard_map.82) | data formatting | bytes 1179648
where the time goes:
time: 42.8 us; the launch traced here: 42.7 us
  Pallas kernels  40.7 us (95%)
  local copies, waits for them, and re-layouts  1.92 us (4%)
    pallas_call x1, Pallas kernels, local(): pl.pallas_call(functools.partial(kernel, n_row, n_col), out_shape=jax.Sha...  40.7 us
    unnamed x1, local copies, waits for them, and re-layouts  1.92 us

commit v1 on v0

--- a/solution.py
+++ b/solution.py
@@ -11,15 +11,29 @@
 LATE = 1
 
 
+GROUP = 4
+STRIP = 16
+
+
+def counted(tiles, blocks, place, count, n_bank, into):
+    code = tiles[pl.ds(place, 1), :] * n_bank + blocks[pl.ds(place, 1), :]
+    slot = lax.broadcasted_iota(jnp.int32, code.shape, 1)
+    code = jnp.where(slot < count, code, -1)
+    shape = (into.shape[0], code.shape[1])
+    hit = lax.broadcasted_iota(jnp.int32, shape, 0) == code
+    times = jnp.sum(jnp.where(hit, 1.0, 0.0).astype(jnp.float32), axis=1, keepdims=True)
+    into[...] = jnp.broadcast_to(times, into.shape)
+
+
 def kernel(
     n_row, n_col,
     a_tiles, a_blocks, a_count, b_tiles, b_blocks, b_count,
     coeff, bank_hbm, out,
-    rows, cols, bank, local_sem, row_send, row_recv, col_send, col_recv,
+    rows, cols, bank, a_fold, b_fold, a_mult, b_mult, local_sem, row_send, row_recv, col_send, col_recv,
 ):
     tile = coeff.shape[0]
     half = tile // 2
-    slots = a_tiles.shape[1]
+    n_bank = bank.shape[0]
     depth, width = n_row // 2, n_col // 2
     row, col = lax.axis_index("row"), lax.axis_index("col")
     z, y = row // 2, row % 2
@@ -137,74 +151,109 @@
             col_copy(own(h), source, h, 0, twin).wait_recv()
             col_copy(part(cols, source, h), source, h, 0, twin).start()
 
+    counted(a_tiles, a_blocks, row, a_count[row], n_bank, a_mult)
+    counted(b_tiles, b_blocks, col, b_count[col], n_bank, b_mult)
+    bank_copy.wait()
+
+    def fold(mult, into, first, place, size):
+        def body(chunk, carry):
+            top = pl.multiple_of(chunk * STRIP, STRIP)
+            totals = [None] * size
+            for b in range(n_bank):
+                block = bank[b, pl.ds(top, STRIP), :].astype(jnp.float32)
+                for g in range(size):
+                    term = mult[pl.ds((first + g) * n_bank + b, 1), :] * block
+                    totals[g] = term if b == 0 else totals[g] + term
+            for g in range(size):
+                high = totals[g].astype(into.dtype)
+                low = (totals[g] - high.astype(jnp.float32)).astype(into.dtype)
+                into[place + g, pl.ds(top, STRIP), :] = high
+                into[place + g, pl.ds(pl.multiple_of(tile + top, STRIP), STRIP), :] = low
+            return carry
+
+        lax.fori_loop(0, tile // STRIP, body, 0)
+
+    def fold_rows(low, high):
+        for first in range(low, high, GROUP):
+            fold(a_mult, a_fold, first, first, min(GROUP, high - first))
+
+    def add_row(which):
+        both = jnp.dot(a_fold[which], rows[which], preferred_element_type=jnp.float32)
+        out[...] += both[:tile] + both[tile:]
+
+    def add_lane(base, d):
+        def body(side, carry):
+            which = base + (2 * side - 1) * 2 * d
+
+            @pl.when(jnp.logical_and(which >= 0, which < n_row))
+            def _():
+                add_row(which)
+
+            return carry
+
+        lax.fori_loop(0, 2, body, 0)
+
+    def await_lane(d):
+        for h in (0, 1):
+            @pl.when(z >= d)
+            def _():
+                arrived(mate - 2 * d, h)
+
+            @pl.when(z + d < depth)
+            def _():
+                arrived(mate + 2 * d, h)
+
+    out[...] = jnp.zeros_like(out)
+    middle = n_row // 2
+    fold_rows(0, middle)
     pass_rows(1, 0)
     pass_cols(0)
+    fold_rows(middle, n_row)
     pass_rows(1, 1)
     pass_cols(1)
-    if depth > 2:
-        pass_rows(2, 0)
-
     own_col.wait()
-    bank_copy.wait()
-    for h in (0, 1):
-        for step in range(width):
-            source = lax.rem(x + step, width) * 2 + 1 - core
-            col_copy(own(h), source, h, 0, twin).wait_recv()
-    out[...] = jnp.zeros_like(out)
-    b_live = b_count[col]
-
-    def add_beta(slot):
-        piece = cols[b_tiles[col, slot]]
-        block = bank[b_blocks[col, slot]]
-        live = jnp.where(slot < b_live, 1.0, 0.0).astype(jnp.float32)
-        out[...] += live * lax.dot_general(
-            piece, block, (((1,), (1,)), ((), ())), preferred_element_type=jnp.float32
-        )
-
-    def beta_range(low, high):
-        def body(slot, carry):
-            add_beta(slot)
+    own_row.wait()
+
+    for first in range(0, n_col, GROUP):
+        size = min(GROUP, n_col - first)
+        fold(b_mult, b_fold, first, 0, size)
+        if first == 0:
+            if depth > 2:
+                pass_rows(2, 0)
+            for h in (0, 1):
+                for step in range(width):
+                    source = lax.rem(x + step, width) * 2 + 1 - core
+                    col_copy(own(h), source, h, 0, twin).wait_recv()
+
+        def add_col(g, carry):
+            both = lax.dot_general(
+                cols[first + g], b_fold[g], (((1,), (1,)), ((), ())),
+                preferred_element_type=jnp.float32,
+            )
+            out[...] += both[:, :tile] + both[:, tile:]
             return carry
-        lax.fori_loop(low, high, body, 0)
-
-    beta_range(0, slots // 3)
+
+        lax.fori_loop(0, size, add_col, 0)
+
+    add_row(row)
     if depth > 2:
         pass_rows(2, 1)
-    else:
-        pass_mate()
-    beta_range(slots // 3, 2 * slots // 3)
-    if depth > 2:
-        pass_mate()
+    pass_mate()
+    add_lane(row, 1)
+    arrived(mate, 1 - LATE)
+    add_row(mate)
     for d in range(3, depth):
         pass_rows(d, 0)
         if d == 3:
-            beta_range(2 * slots // 3, slots)
+            add_lane(row, 2)
         pass_rows(d, 1)
-    if depth <= 3:
-        beta_range(2 * slots // 3, slots)
-
-    own_row.wait()
-    arrived(mate, 1 - LATE)
+    if depth == 3:
+        add_lane(row, 2)
     for d in range(1, depth):
-        for h in (0, 1):
-            @pl.when(z >= d)
-            def _():
-                arrived(mate - 2 * d, h)
-
-            @pl.when(z + d < depth)
-            def _():
-                arrived(mate + 2 * d, h)
-
-    a_live = a_count[row]
-
-    def add_alpha(slot, carry):
-        piece = rows[a_tiles[row, slot]]
-        block = bank[a_blocks[row, slot]]
-        live = jnp.where(slot < a_live, 1.0, 0.0).astype(jnp.float32)
-        out[...] += live * jnp.dot(block, piece, preferred_element_type=jnp.float32)
-        return carry
-
-    lax.fori_loop(0, slots, add_alpha, 0)
+        await_lane(d)
+        if d >= 3:
+            add_lane(row, d)
+        add_lane(mate, d)
 
     def sent_row(which, h, way):
         row_copy(own(h), which, h, way, mate).wait_send()
@@ -261,13 +310,17 @@
         return pl.pallas_call(
             functools.partial(kernel, n_row, n_col),
             out_shape=jax.ShapeDtypeStruct((tile, tile), jnp.float32),
-            in_specs=[pl.BlockSpec(memory_space=pltpu.SMEM)] * 6
+            in_specs=([pl.BlockSpec(memory_space=pltpu.VMEM)] * 2 + [pl.BlockSpec(memory_space=pltpu.SMEM)]) * 2
             + [pl.BlockSpec(memory_space=pltpu.HBM)] * 2,
             out_specs=pl.BlockSpec(memory_space=pltpu.VMEM),
             scratch_shapes=[
                 pltpu.VMEM((n_row, tile, tile), coeff.dtype),
                 pltpu.VMEM((n_col, tile, tile), coeff.dtype),
                 pltpu.VMEM(bank.shape, bank.dtype),
+                pltpu.VMEM((n_row, 2 * tile, tile), bank.dtype),
+                pltpu.VMEM((min(GROUP, n_col), 2 * tile, tile), bank.dtype),
+                pltpu.VMEM((n_row * bank.shape[0], tile), jnp.float32),
+                pltpu.VMEM((n_col * bank.shape[0], tile), jnp.float32),
                 pltpu.SemaphoreType.DMA((3,)),
                 pltpu.SemaphoreType.DMA((3, n_row, 2)),
                 pltpu.SemaphoreType.DMA((n_row, 2)),

time: 42.8 us -> 36.1 us (0.84)
  Pallas kernels: 40.7 us -> 34 us
    pallas_call x1, Pallas kernels: 40.7 us -> 34 us  [local(): pl.pallas_call(functools.partial(kernel, n_row, n_col), out_shape=jax.Sha...]
where the time goes in v1:
time: 36.1 us; the launch traced here: 35.9 us
  Pallas kernels  34 us (94%)
  local copies, waits for them, and re-layouts  1.92 us (5%)
    pallas_call x1, Pallas kernels, local(): pl.pallas_call(functools.partial(kernel, n_row, n_col), out_shape=jax.Sha...  34 us
    unnamed x1, local copies, waits for them, and re-layouts  1.92 us

profile of v1, /device:TPU:0, one launch (start us, length us, event | category | flops | bytes accessed | tf_op | source)
XLA Modules:
  0.0 35.9 jit_solution(5575623662324827081)
XLA Ops:
  0.0 34.0 %shard_map.82 = f32[384,384]{1,0:T(8,128)} custom-call(s32[8,24]{1,0:T(8,128)} %a_tiles.1, s32[8,24]{1,0:T(8,128)} %a_blocks.1, s32[8]{0:T(128)} %a_count.1, s32[4,24]{1,0:T(4,128)} %b_tiles.1, s32[4,24]{1,0:T(4,128)} %b_blocks.1, s32[4]{0:T(128)} %b_count.1, bf16[384,384]{1,0:T(8,128)(2,1)} %coeff.1, bf16[16,384,384]{2,1,0:T(8,128)(2,1)} %bank_hbm.1), custom_call_target="tpu_custom_call" | custom-call | flops 5435817984 | bytes 5603328 | tf_op jit(solution)/shard_map/pallas_call | solution.py:310
  34.0 1.9 %copy.10 = f32[384,384]{1,0:T(8,128)} copy(f32[384,384]{1,0:T(8,128)} %shard_map.82) | data formatting | bytes 1179648

commit v2 on v1

--- a/solution.py
+++ b/solution.py
@@ -8,7 +8,8 @@
 from jax.sharding import PartitionSpec as P
 
 MESH = pl.DeviceIdType.MESH
-LATE = 1
+PARTS = 2
+RELAY = (1,)
 
 
 GROUP = 4
@@ -28,11 +29,11 @@
 def kernel(
     n_row, n_col,
     a_tiles, a_blocks, a_count, b_tiles, b_blocks, b_count,
-    coeff, bank_hbm, out,
-    rows, cols, bank, a_fold, b_fold, a_mult, b_mult, local_sem, row_send, row_recv, col_send, col_recv,
+    coeff, bank_hbm, out, beta_hbm,
+    rows, cols, bank, a_fold, b_fold, a_mult, b_mult, beta, local_sem, row_send, row_recv, col_send, col_recv,
 ):
     tile = coeff.shape[0]
-    half = tile // 2
+    half = tile // PARTS
     n_bank = bank.shape[0]
     depth, width = n_row // 2, n_col // 2
     row, col = lax.axis_index("row"), lax.axis_index("col")
@@ -95,7 +96,7 @@
 
     UP, DOWN, SIDE = 0, 1, 2
 
-    for h in (0, 1):
+    for h in range(PARTS):
         @pl.when(has_up)
         def _():
             row_copy(own(h), row, h, UP, row + 2).start()
@@ -109,6 +110,20 @@
             col_copy(own(h), col, h, step, lax.rem(x + step, width) * 2 + core).start()
         col_copy(own(h), col, h, 0, twin).start()
 
+    chained = depth > 2
+
+    def to_mate(which, d, h, beside_end):
+        if chained and d == depth - 1 and h in RELAY:
+            return
+
+        def go():
+            row_copy(part(rows, which, h), which, h, SIDE, mate).start()
+
+        if chained and d == 1:
+            pl.when(jnp.logical_not(beside_end))(go)
+        else:
+            go()
+
     def pass_rows(d, h):
         below, above = row - 2 * d, row + 2 * d
 
@@ -120,8 +135,7 @@
             def _():
                 row_copy(part(rows, below, h), below, h, UP, row + 2).start()
 
-            if d != 1 or h != LATE:
-                row_copy(part(rows, below, h), below, h, SIDE, mate).start()
+            to_mate(below, d, h, z == 1)
 
         @pl.when(z + d < depth)
         def _():
@@ -131,19 +145,37 @@
             def _():
                 row_copy(part(rows, above, h), above, h, DOWN, row - 2).start()
 
-            if d != 1 or h != LATE:
-                row_copy(part(rows, above, h), above, h, SIDE, mate).start()
-
-    def pass_mate():
-        arrived(mate, LATE)
-
-        @pl.when(has_up)
-        def _():
-            row_copy(part(rows, mate, LATE), mate, LATE, UP, row + 2).start()
-
-        @pl.when(has_down)
-        def _():
-            row_copy(part(rows, mate, LATE), mate, LATE, DOWN, row - 2).start()
+            to_mate(above, d, h, z == depth - 2)
+
+    def pass_mate(h):
+        if not chained:
+            return
+
+        @pl.when(z == 0)
+        def _():
+            arrived(mate, h)
+            row_copy(part(rows, mate, h), mate, h, UP, row + 2).start()
+
+        @pl.when(z == depth - 1)
+        def _():
+            arrived(mate, h)
+            row_copy(part(rows, mate, h), mate, h, DOWN, row - 2).start()
+
+    far_high, far_low = mate + 2 * (depth - 1 - z), mate - 2 * z
+
+    def relay(h):
+        if not chained:
+            return
+
+        @pl.when(z == 1)
+        def _():
+            arrived(far_high, h)
+            row_copy(part(rows, far_high, h), far_high, h, DOWN, row - 2).start()
+
+        @pl.when(z == depth - 2)
+        def _():
+            arrived(far_low, h)
+            row_copy(part(rows, far_low, h), far_low, h, UP, row + 2).start()
 
     def pass_cols(h):
         for step in range(1, width):
@@ -193,8 +225,32 @@
 
         lax.fori_loop(0, 2, body, 0)
 
-    def await_lane(d):
-        for h in (0, 1):
+    def await_mate(d):
+        for h in range(PARTS):
+            if chained and h in RELAY:
+                if d == 0:
+                    @pl.when(jnp.logical_and(z > 0, z < depth - 1))
+                    def _():
+                        arrived(mate, h)
+                    continue
+                if d == depth - 2:
+                    @pl.when(jnp.logical_and(z >= d, z != depth - 2))
+                    def _():
+                        arrived(mate - 2 * d, h)
+
+                    @pl.when(jnp.logical_and(z + d < depth, z != 1))
+                    def _():
+                        arrived(mate + 2 * d, h)
+                    continue
+            if d == 0:
+                if chained:
+                    @pl.when(jnp.logical_and(z > 0, z < depth - 1))
+                    def _():
+                        arrived(mate, h)
+                else:
+                    arrived(mate, h)
+                continue
+
             @pl.when(z >= d)
             def _():
                 arrived(mate - 2 * d, h)
@@ -204,13 +260,20 @@
                 arrived(mate + 2 * d, h)
 
     out[...] = jnp.zeros_like(out)
+    beta[...] = jnp.zeros_like(beta)
     middle = n_row // 2
     fold_rows(0, middle)
-    pass_rows(1, 0)
-    pass_cols(0)
+    for h in range(PARTS // 2):
+        if depth > 1:
+            pass_rows(1, h)
+        pass_mate(h)
+        pass_cols(h)
     fold_rows(middle, n_row)
-    pass_rows(1, 1)
-    pass_cols(1)
+    for h in range(PARTS // 2, PARTS):
+        if depth > 1:
+            pass_rows(1, h)
+        pass_mate(h)
+        pass_cols(h)
     own_col.wait()
     own_row.wait()
 
@@ -218,9 +281,10 @@
         size = min(GROUP, n_col - first)
         fold(b_mult, b_fold, first, 0, size)
         if first == 0:
-            if depth > 2:
-                pass_rows(2, 0)
-            for h in (0, 1):
+            if depth > 3:
+                for h in range(PARTS // 2):
+                    pass_rows(2, h)
+            for h in range(PARTS):
                 for step in range(width):
                     source = lax.rem(x + step, width) * 2 + 1 - core
                     col_copy(own(h), source, h, 0, twin).wait_recv()
@@ -230,35 +294,44 @@
                 cols[first + g], b_fold[g], (((1,), (1,)), ((), ())),
                 preferred_element_type=jnp.float32,
             )
-            out[...] += both[:, :tile] + both[:, tile:]
+            beta[...] += both[:, :tile] + both[:, tile:]
             return carry
 
         lax.fori_loop(0, size, add_col, 0)
 
+    beta_copy = pltpu.make_async_copy(beta, beta_hbm, local_sem.at[3])
+    beta_copy.start()
     add_row(row)
+    if depth > 3:
+        for h in range(PARTS // 2, PARTS):
+            pass_rows(2, h)
+    if depth > 1:
+        add_lane(row, 1)
+    await_mate(0)
+    add_row(mate)
+    for d in range(3, depth - 1):
+        for h in range(PARTS):
+            pass_rows(d, h)
+    for h in RELAY:
+        relay(h)
     if depth > 2:
-        pass_rows(2, 1)
-    pass_mate()
-    add_lane(row, 1)
-    arrived(mate, 1 - LATE)
-    add_row(mate)
-    for d in range(3, depth):
-        pass_rows(d, 0)
-        if d == 3:
+        for h in range(PARTS // 2):
+            pass_rows(depth - 1, h)
+        if depth > 3:
             add_lane(row, 2)
-        pass_rows(d, 1)
-    if depth == 3:
-        add_lane(row, 2)
+        for h in range(PARTS // 2, PARTS):
+            pass_rows(depth - 1, h)
     for d in range(1, depth):
-        await_lane(d)
-        if d >= 3:
+        if d == depth - 1 and d > 1 or d > 2:
             add_lane(row, d)
+        await_mate(d)
         add_lane(mate, d)
 
+    beta_copy.wait()
     def sent_row(which, h, way):
         row_copy(own(h), which, h, way, mate).wait_send()
 
-    for h in (0, 1):
+    for h in range(PARTS):
         @pl.when(has_up)
         def _():
             sent_row(row, h, UP)
@@ -274,14 +347,21 @@
             source = lax.rem(x + step, width) * 2 + core
             col_copy(own(h), source, h, 0, twin).wait_send()
         for d in range(1, depth):
+            def left_for_mate(which, beside_end):
+                if chained and d == depth - 1 and h in RELAY:
+                    return
+                if chained and d == 1:
+                    pl.when(jnp.logical_not(beside_end))(lambda: sent_row(which, h, SIDE))
+                else:
+                    sent_row(which, h, SIDE)
+
             @pl.when(z >= d)
             def _():
                 @pl.when(has_up)
                 def _():
                     sent_row(row - 2 * d, h, UP)
 
-                if d != 1 or h != LATE:
-                    sent_row(row - 2 * d, h, SIDE)
+                left_for_mate(row - 2 * d, z == 1)
 
             @pl.when(z + d < depth)
             def _():
@@ -289,16 +369,28 @@
                 def _():
                     sent_row(row + 2 * d, h, DOWN)
 
-                if d != 1 or h != LATE:
-                    sent_row(row + 2 * d, h, SIDE)
-
-    @pl.when(has_up)
-    def _():
-        sent_row(mate, LATE, UP)
-
-    @pl.when(has_down)
-    def _():
-        sent_row(mate, LATE, DOWN)
+                left_for_mate(row + 2 * d, z == depth - 2)
+
+    if chained:
+        @pl.when(z == 0)
+        def _():
+            for h in range(PARTS):
+                sent_row(mate, h, UP)
+
+        @pl.when(z == depth - 1)
+        def _():
+            for h in range(PARTS):
+                sent_row(mate, h, DOWN)
+
+        @pl.when(z == 1)
+        def _():
+            for h in RELAY:
+                sent_row(far_high, h, DOWN)
+
+        @pl.when(z == depth - 2)
+        def _():
+            for h in RELAY:
+                sent_row(far_low, h, UP)
 
 
 def solution(mesh):
@@ -307,12 +399,12 @@
     def local(coeff, bank, a_tiles, a_blocks, a_count, b_tiles, b_blocks, b_count):
         tile = coeff.shape[0]
         flops = 2 * (a_tiles.shape[1] + b_tiles.shape[1]) * tile**3
-        return pl.pallas_call(
+        sigma_alpha, sigma_beta = pl.pallas_call(
             functools.partial(kernel, n_row, n_col),
-            out_shape=jax.ShapeDtypeStruct((tile, tile), jnp.float32),
+            out_shape=[jax.ShapeDtypeStruct((tile, tile), jnp.float32)] * 2,
             in_specs=([pl.BlockSpec(memory_space=pltpu.VMEM)] * 2 + [pl.BlockSpec(memory_space=pltpu.SMEM)]) * 2
             + [pl.BlockSpec(memory_space=pltpu.HBM)] * 2,
-            out_specs=pl.BlockSpec(memory_space=pltpu.VMEM),
+            out_specs=[pl.BlockSpec(memory_space=pltpu.VMEM), pl.BlockSpec(memory_space=pltpu.HBM)],
             scratch_shapes=[
                 pltpu.VMEM((n_row, tile, tile), coeff.dtype),
                 pltpu.VMEM((n_col, tile, tile), coeff.dtype),
@@ -321,11 +413,12 @@
                 pltpu.VMEM((min(GROUP, n_col), 2 * tile, tile), bank.dtype),
                 pltpu.VMEM((n_row * bank.shape[0], tile), jnp.float32),
                 pltpu.VMEM((n_col * bank.shape[0], tile), jnp.float32),
-                pltpu.SemaphoreType.DMA((3,)),
-                pltpu.SemaphoreType.DMA((3, n_row, 2)),
-                pltpu.SemaphoreType.DMA((n_row, 2)),
-                pltpu.SemaphoreType.DMA((max(1, n_col // 2), n_col, 2)),
-                pltpu.SemaphoreType.DMA((n_col, 2)),
+                pltpu.VMEM((tile, tile), jnp.float32),
+                pltpu.SemaphoreType.DMA((4,)),
+                pltpu.SemaphoreType.DMA((3, n_row, PARTS)),
+                pltpu.SemaphoreType.DMA((n_row, PARTS)),
+                pltpu.SemaphoreType.DMA((max(1, n_col // 2), n_col, PARTS)),
+                pltpu.SemaphoreType.DMA((n_col, PARTS)),
             ],
             compiler_params=pltpu.CompilerParams(
                 collective_id=0, has_side_effects=True, vmem_limit_bytes=62 * 1024 * 1024
@@ -334,6 +427,7 @@
                 flops=flops, bytes_accessed=bank.size * 2 + tile * tile * 6, transcendentals=0
             ),
         )(a_tiles, a_blocks, a_count, b_tiles, b_blocks, b_count, coeff, bank)
+        return sigma_alpha + sigma_beta
 
     return jax.shard_map(
         local,

time: 36.1 us -> 34.2 us (0.947)
  other arithmetic: 0 us -> 2.12 us
  Pallas kernels: 34 us -> 31.9 us
  local copies, waits for them, and re-layouts: 1.92 us -> 0 us
    add x0 -> x1, other arithmetic: none -> 2.12 us  [local(): return sigma_alpha + sigma_beta]
    pallas_call x1, Pallas kernels: 34 us -> 31.9 us  [local(): pl.pallas_call(functools.partial(kernel, n_row, n_col), out_shape=[jax.Sh...]
    unnamed x1 -> x0, local copies, waits for them, and re-layouts: 1.92 us -> none
where the time goes in v2:
time: 34.2 us; the launch traced here: 34.1 us
  Pallas kernels  31.9 us (93%)
  other arithmetic  2.12 us (6%)
    pallas_call x1, Pallas kernels, local(): pl.pallas_call(functools.partial(kernel, n_row, n_col), out_shape=[jax.Sh...  31.9 us
    add x1, other arithmetic, local(): return sigma_alpha + sigma_beta  2.12 us

profile of v2, /device:TPU:0, one launch (start us, length us, event | category | flops | bytes accessed | tf_op | source)
XLA Modules:
  0.0 34.1 jit_solution(3322220000421848151)
XLA Ops:
  0.0 31.9 %shard_map.82 = (f32[384,384]{1,0:T(8,128)}, f32[384,384]{1,0:T(8,128)}) custom-call(s32[8,24]{1,0:T(8,128)} %a_tiles.1, s32[8,24]{1,0:T(8,128)} %a_blocks.1, s32[8]{0:T(128)} %a_count.1, s32[4,24]{1,0:T(4,128)} %b_tiles.1, s32[4,24]{1,0:T(4,128)} %b_blocks.1, s32[4]{0:T(128)} %b_count.1, bf16[384,384]{1,0:T(8,128)(2,1)} %coeff.1, bf16[16,384,384]{2,1,0:T(8,128)(2,1)} %bank_hbm.1), custom_call_target="tpu_custom_call" | custom-call | flops 5435817984 | bytes 5603328 | tf_op jit(solution)/shard_map/pallas_call | solution.py:402
  31.9 2.1 %add.3 = f32[384,384]{1,0:T(8,128)} add(f32[384,384]{1,0:T(8,128)} %get-tuple-element.7, f32[384,384]{1,0:T(8,128)} %get-tuple-element.8) | non-fusion elementwise | flops 147456 | bytes 1769472 | tf_op jit(solution)/shard_map/add | solution.py:430

commit v3 on v2

--- a/solution.py
+++ b/solution.py
@@ -29,8 +29,8 @@
 def kernel(
     n_row, n_col,
     a_tiles, a_blocks, a_count, b_tiles, b_blocks, b_count,
-    coeff, bank_hbm, out, beta_hbm,
-    rows, cols, bank, a_fold, b_fold, a_mult, b_mult, beta, local_sem, row_send, row_recv, col_send, col_recv,
+    coeff, bank_hbm, out,
+    rows, cols, bank, a_fold, b_fold, a_mult, b_mult, local_sem, row_send, row_recv, col_send, col_recv,
 ):
     tile = coeff.shape[0]
     half = tile // PARTS
@@ -260,7 +260,6 @@
                 arrived(mate + 2 * d, h)
 
     out[...] = jnp.zeros_like(out)
-    beta[...] = jnp.zeros_like(beta)
     middle = n_row // 2
     fold_rows(0, middle)
     for h in range(PARTS // 2):
@@ -294,13 +293,11 @@
                 cols[first + g], b_fold[g], (((1,), (1,)), ((), ())),
                 preferred_element_type=jnp.float32,
             )
-            beta[...] += both[:, :tile] + both[:, tile:]
+            out[...] += both[:, :tile] + both[:, tile:]
             return carry
 
         lax.fori_loop(0, size, add_col, 0)
 
-    beta_copy = pltpu.make_async_copy(beta, beta_hbm, local_sem.at[3])
-    beta_copy.start()
     add_row(row)
     if depth > 3:
         for h in range(PARTS // 2, PARTS):
@@ -327,7 +324,6 @@
         await_mate(d)
         add_lane(mate, d)
 
-    beta_copy.wait()
     def sent_row(which, h, way):
         row_copy(own(h), which, h, way, mate).wait_send()
 
@@ -399,12 +395,12 @@
     def local(coeff, bank, a_tiles, a_blocks, a_count, b_tiles, b_blocks, b_count):
         tile = coeff.shape[0]
         flops = 2 * (a_tiles.shape[1] + b_tiles.shape[1]) * tile**3
-        sigma_alpha, sigma_beta = pl.pallas_call(
+        return pl.pallas_call(
             functools.partial(kernel, n_row, n_col),
-            out_shape=[jax.ShapeDtypeStruct((tile, tile), jnp.float32)] * 2,
+            out_shape=jax.ShapeDtypeStruct((tile, tile), jnp.float32),
             in_specs=([pl.BlockSpec(memory_space=pltpu.VMEM)] * 2 + [pl.BlockSpec(memory_space=pltpu.SMEM)]) * 2
             + [pl.BlockSpec(memory_space=pltpu.HBM)] * 2,
-            out_specs=[pl.BlockSpec(memory_space=pltpu.VMEM), pl.BlockSpec(memory_space=pltpu.HBM)],
+            out_specs=pl.BlockSpec(memory_space=pltpu.VMEM),
             scratch_shapes=[
                 pltpu.VMEM((n_row, tile, tile), coeff.dtype),
                 pltpu.VMEM((n_col, tile, tile), coeff.dtype),
@@ -413,8 +409,7 @@
                 pltpu.VMEM((min(GROUP, n_col), 2 * tile, tile), bank.dtype),
                 pltpu.VMEM((n_row * bank.shape[0], tile), jnp.float32),
                 pltpu.VMEM((n_col * bank.shape[0], tile), jnp.float32),
-                pltpu.VMEM((tile, tile), jnp.float32),
-                pltpu.SemaphoreType.DMA((4,)),
+                pltpu.SemaphoreType.DMA((3,)),
                 pltpu.SemaphoreType.DMA((3, n_row, PARTS)),
                 pltpu.SemaphoreType.DMA((n_row, PARTS)),
                 pltpu.SemaphoreType.DMA((max(1, n_col // 2), n_col, PARTS)),
@@ -427,7 +422,6 @@
                 flops=flops, bytes_accessed=bank.size * 2 + tile * tile * 6, transcendentals=0
             ),
         )(a_tiles, a_blocks, a_count, b_tiles, b_blocks, b_count, coeff, bank)
-        return sigma_alpha + sigma_beta
 
     return jax.shard_map(
         local,

time: 34.2 us -> 34 us (level)
  other arithmetic: 2.12 us -> 0 us
  local copies, waits for them, and re-layouts: 0 us -> 1.92 us
    add x1 -> x0, other arithmetic: 2.12 us -> none  [local(): return sigma_alpha + sigma_beta]
    unnamed x0 -> x1, local copies, waits for them, and re-layouts: none -> 1.92 us
where the time goes in v3:
time: 34 us; the launch traced here: 33.8 us
  Pallas kernels  31.9 us (94%)
  local copies, waits for them, and re-layouts  1.92 us (6%)
    pallas_call x1, Pallas kernels, local(): pl.pallas_call(functools.partial(kernel, n_row, n_col), out_shape=jax.Sha...  31.9 us
    unnamed x1, local copies, waits for them, and re-layouts  1.92 us

profile of v3, /device:TPU:0, one launch (start us, length us, event | category | flops | bytes accessed | tf_op | source)
XLA Modules:
  0.0 33.8 jit_solution(9643223242136415266)
XLA Ops:
  0.0 31.9 %shard_map.82 = f32[384,384]{1,0:T(8,128)} custom-call(s32[8,24]{1,0:T(8,128)} %a_tiles.1, s32[8,24]{1,0:T(8,128)} %a_blocks.1, s32[8]{0:T(128)} %a_count.1, s32[4,24]{1,0:T(4,128)} %b_tiles.1, s32[4,24]{1,0:T(4,128)} %b_blocks.1, s32[4]{0:T(128)} %b_count.1, bf16[384,384]{1,0:T(8,128)(2,1)} %coeff.1, bf16[16,384,384]{2,1,0:T(8,128)(2,1)} %bank_hbm.1), custom_call_target="tpu_custom_call" | custom-call | flops 5435817984 | bytes 5603328 | tf_op jit(solution)/shard_map/pallas_call | solution.py:398
  31.9 1.9 %copy.10 = f32[384,384]{1,0:T(8,128)} copy(f32[384,384]{1,0:T(8,128)} %shard_map.82) | data formatting | bytes 1179648
